TPU v7x, 32 devices: a whole 2x2x4 slice. The times are simulated.
32 devices in a mesh: tok: 8 (over z, y), ffn: 4 (over x, core).
Axes of the slice: x: 2, y: 2, z: 4, core: 2. Of those that a mesh axis runs over, the one named last changes fastest.
Arguments:
- enc_in: bfloat16 [5120, 768], P(('tok', 'ffn')), may hold values from -6 to 6
- dec_in: bfloat16 [5120, 768], P(('tok', 'ffn')), may hold values from -6 to 6
- cotangent: bfloat16 [5120, 768], P(('tok', 'ffn')), may hold values from -6 to 6
- enc_lengths: int32 [8, 5], P('tok'), may hold values from 1 to 512, 640 in all within a row
- dec_lengths: int32 [8, 5], P('tok'), may hold values from 16 to 114, as said below
- qk_weights: bfloat16 [3, 2, 768, 768], replicated, may hold values from -0.109375 to 0.109375
- v_weights: bfloat16 [3, 768, 768], replicated, may hold values from -0.21875 to 0.21875
- out_weights: bfloat16 [3, 768, 768], replicated, may hold values from -0.875 to 0.875
- ffn_in: bfloat16 [2, 768, 3072], P(None, None, 'ffn'), may hold values from -0.21875 to 0.21875
- ffn_out: bfloat16 [2, 3072, 768], P(None, 'ffn'), may hold values from -0.15625 to 0.15625
- bias_tables: float32 [2, 32, 12], replicated, may hold values from -4 to 4
- gains: float32 [6, 768], replicated, may hold values from 0.5 to 1.5
Outputs:
- dec_out: bfloat16 [5120, 768], P(('tok', 'ffn'))
- enc_grad: bfloat16 [5120, 768], P(('tok', 'ffn'))
- dec_grad: bfloat16 [5120, 768], P(('tok', 'ffn'))
- qk_grads: float32 [3, 2, 768, 768], P(None, None, 'tok', 'ffn')
- v_grads: float32 [3, 768, 768], P(None, 'tok', 'ffn')
- out_grads: float32 [3, 768, 768], P(None, 'ffn', 'tok')
- ffn_in_grads: float32 [2, 768, 3072], P(None, 'tok', 'ffn')
- ffn_out_grads: float32 [2, 3072, 768], P(None, 'ffn', 'tok')
- table_grads: float32 [2, 32, 12], replicated
- gain_grads: float32 [6, 768], replicated
- final_gain_grad: float32 [768], replicated
Inputs may be any that keep to these rules, and one draw needn't show every extreme that they name: `enc_lengths`: in each pack the 5 example lengths sum to 640, and the longest is exactly 512. `dec_lengths`: in each pack one example's target has exactly 114 tokens.
All inputs are finite; a program needn't handle non-finite values.
Results may differ from a plain program's by a relative error of at most 0.028.
Values may be sent and summed in bfloat16 or wider, within the bound.
A program may use at most 320 MiB of HBM per device.

v0:
```python
import jax
import jax.numpy as jnp
from jax import lax
from jax.sharding import PartitionSpec as P

DH = 64
BUCKETS = 32
SLOT = 128


norm_epsilon = 1e-06
masked_score = -1000000000.0
wide_limits = (12, 16, 23, 32, 46, 64, 91)
causal_limits = (19, 21, 24, 27, 31, 35, 40, 46, 52, 59, 67, 77, 87, 99, 113)
contract_rows = (((0,), (0,)), ((), ()))
contract_last = (((1,), (1,)), ((), ()))
contract_plain = (((1,), (0,)), ((), ()))


def bucket_index(relative, causal):
    if causal:
        distance = jnp.maximum(-relative, 0)
        limits = jnp.array(causal_limits, dtype=jnp.int32)
        far = 16 + jnp.sum((distance[..., None] >= limits).astype(jnp.int32), axis=-1)
        return jnp.where(distance < 16, distance, far)
    distance = jnp.abs(relative)
    limits = jnp.array(wide_limits, dtype=jnp.int32)
    far = 8 + jnp.sum((distance[..., None] >= limits).astype(jnp.int32), axis=-1)
    return jnp.where(distance < 8, distance, far) + 16 * (relative > 0).astype(jnp.int32)


def rms_scale(values, gain_vector):
    return (
        values
        * lax.rsqrt(jnp.mean(values * values, axis=-1, keepdims=True) + norm_epsilon)
        * gain_vector
    )


def norm_back(values, gain_vector, grad_normed):
    normed_value, norm_pull = jax.vjp(rms_scale, values, gain_vector)
    return norm_pull(grad_normed)


def gelu_exact(values):
    return jax.nn.gelu(values, approximate=False)


def gelu_slope(values):
    unused_value, slope_pull = jax.vjp(gelu_exact, values)
    return slope_pull(jnp.ones_like(values))[0]


def product(left, right, contract):
    return lax.dot_general(left, right, contract, preferred_element_type=jnp.float32)


def bias_block(table_part, first_row, block_rows, key_count, causal):
    line_width = block_rows + key_count
    relative = jnp.arange(line_width, dtype=jnp.int32) - (block_rows - 1) - first_row
    onehot = (
        bucket_index(relative, causal)[:, None] == jnp.arange(BUCKETS, dtype=jnp.int32)[None, :]
    ).astype(jnp.float32)
    bias_line = jnp.dot(onehot, table_part, precision=lax.Precision.HIGHEST).T
    head_count = bias_line.shape[0]
    spread = jnp.broadcast_to(bias_line[:, None, :], (head_count, block_rows, line_width)).reshape(
        head_count, block_rows * line_width
    )
    skewed = spread[:, : block_rows * (line_width - 1)].reshape(
        head_count, block_rows, line_width - 1
    )
    return skewed[:, :, block_rows - 1 : block_rows - 1 + key_count]


def attend(query, key_proj, value_proj, live_of, table_part, causal):
    row_count = query.shape[0]
    key_count = key_proj.shape[0]
    head_count = query.shape[1] // DH
    keys_split = key_proj.reshape(key_count, head_count, DH)
    values_split = value_proj.reshape(key_count, head_count, DH)

    def one_block(block_index):
        first_row = block_index * row_count
        query_block = query.reshape(row_count, head_count, DH)
        scores = jnp.einsum(
            "qhd,khd->hqk", query_block, keys_split, preferred_element_type=jnp.float32
        )
        if table_part is not None:
            scores = scores + bias_block(table_part, first_row, row_count, key_count, causal)
        scores = jnp.where(live_of(first_row, row_count)[None], scores, masked_score)
        row_max = jnp.max(scores, axis=-1, keepdims=True)
        raised = jnp.exp(scores - row_max)
        row_total = jnp.sum(raised, axis=-1, keepdims=True)
        weights_low = (raised / row_total).astype(jnp.bfloat16)
        mixed = jnp.einsum(
            "hqk,khd->qhd", weights_low, values_split, preferred_element_type=jnp.float32
        )
        return (
            mixed.astype(jnp.bfloat16).reshape(row_count, head_count * DH),
            (row_max + jnp.log(row_total))[:, :, 0],
        )

    mixed, log_totals = lax.map(one_block, jnp.arange(row_count // row_count, dtype=jnp.int32))
    return (mixed.reshape(row_count, head_count * DH), log_totals)


def attend_back(query, key_proj, value_proj, log_totals, grad_mixed, live_of, table_part, causal):
    row_count = query.shape[0]
    key_count = key_proj.shape[0]
    head_count = query.shape[1] // DH
    keys_split = key_proj.reshape(key_count, head_count, DH)
    values_split = value_proj.reshape(key_count, head_count, DH)

    def one_block(carry, block_index):
        grad_keys, grad_values, grad_table = carry
        first_row = block_index * row_count
        query_block = query.reshape(row_count, head_count, DH)
        grad_block = grad_mixed.reshape(row_count, head_count, DH)
        scores = jnp.einsum(
            "qhd,khd->hqk", query_block, keys_split, preferred_element_type=jnp.float32
        )
        if table_part is not None:
            bias, table_pull = jax.vjp(
                lambda table_arg: bias_block(table_arg, first_row, row_count, key_count, causal),
                table_part,
            )
            scores = scores + bias
        live_mask = live_of(first_row, row_count)[None]
        scores = jnp.where(live_mask, scores, masked_score)
        weights = jnp.where(live_mask, jnp.exp(scores - log_totals[block_index][:, :, None]), 0.0)
        grad_weights = jnp.einsum(
            "qhd,khd->hqk", grad_block, values_split, preferred_element_type=jnp.float32
        )
        row_dot = jnp.sum(weights * grad_weights, axis=-1, keepdims=True)
        grad_scores = (weights * (grad_weights - row_dot)).astype(jnp.bfloat16)
        grad_query = jnp.einsum(
            "hqk,khd->qhd", grad_scores, keys_split, preferred_element_type=jnp.float32
        )
        grad_keys = grad_keys + jnp.einsum(
            "hqk,qhd->khd", grad_scores, query_block, preferred_element_type=jnp.float32
        )
        grad_values = grad_values + jnp.einsum(
            "hqk,qhd->khd",
            weights.astype(jnp.bfloat16),
            grad_block,
            preferred_element_type=jnp.float32,
        )
        if table_part is not None:
            grad_table = grad_table + table_pull(grad_scores.astype(jnp.float32))[0]
        return (
            (grad_keys, grad_values, grad_table),
            grad_query.astype(jnp.bfloat16).reshape(row_count, head_count * DH),
        )

    start_carry = (
        jnp.zeros((key_count, head_count, DH), jnp.float32),
        jnp.zeros((key_count, head_count, DH), jnp.float32),
        jnp.zeros((BUCKETS, head_count), jnp.float32),
    )
    final_carry, grad_query = lax.scan(
        one_block, start_carry, jnp.arange(row_count // row_count, dtype=jnp.int32)
    )
    grad_keys, grad_values, grad_table = final_carry
    return (
        grad_query.reshape(row_count, head_count * DH),
        grad_keys.astype(jnp.bfloat16).reshape(key_count, head_count * DH),
        grad_values.astype(jnp.bfloat16).reshape(key_count, head_count * DH),
        grad_table,
    )


def on_device(
    enc_in,
    dec_in,
    cotangent,
    enc_lengths,
    dec_lengths,
    qk_weights,
    v_weights,
    out_weights,
    ffn_in,
    ffn_out,
    bias_tables,
    gains,
):
    group_size = lax.axis_size("ffn")
    group_index = lax.axis_index("ffn")
    token_groups = lax.axis_size("tok")
    row_count = enc_in.shape[0]
    packed = row_count * group_size
    model_width = enc_in.shape[1]
    full_width = qk_weights.shape[3]
    local_width = full_width // group_size
    local_heads = local_width // DH
    positions = jnp.arange(packed, dtype=jnp.int32)
    lengths_here = enc_lengths[0]
    example_ends = jnp.cumsum(lengths_here)
    enc_segment = (
        jnp.sum(
            (positions[:, None] >= (example_ends - lengths_here)[None, :]).astype(jnp.int32), axis=1
        )
        - 1
    )
    dec_segment = positions // SLOT
    example_ids = jnp.arange(dec_lengths.shape[1], dtype=jnp.int32)
    slot_length = jnp.sum(
        jnp.where(dec_segment[:, None] == example_ids[None, :], dec_lengths[0][None, :], 0), axis=1
    )
    dec_valid = positions % SLOT < slot_length
    enc_table = lax.dynamic_slice_in_dim(bias_tables[0], group_index * local_heads, local_heads, 1)
    dec_table = lax.dynamic_slice_in_dim(bias_tables[1], group_index * local_heads, local_heads, 1)

    def enc_live(first_row, block_rows):
        return enc_segment[:, None] == enc_segment[None, :]

    def self_live(first_row, block_rows):
        query_place = first_row + jnp.arange(block_rows, dtype=jnp.int32)
        return (
            (dec_segment[:, None] == dec_segment[None, :])
            & (positions[None, :] <= query_place[:, None])
            & dec_valid[None, :]
        )

    def cross_live(first_row, block_rows):
        return dec_segment[:, None] == enc_segment[None, :]

    def ffn_rows(values):
        return lax.all_gather(values, "ffn", axis=0, tiled=True)

    def ffn_sum(left, right, contract):
        return lax.psum_scatter(
            product(left, right, contract).astype(jnp.bfloat16),
            "ffn",
            scatter_dimension=0,
            tiled=True,
        ).astype(jnp.float32)

    def attention_forward(layer_index, source_q, source_kv, live_of, table_part, causal):
        w_query = qk_weights[layer_index, 0]
        w_key = qk_weights[layer_index, 1]
        w_value = v_weights[layer_index]
        w_out = out_weights[layer_index]
        query = jnp.dot(source_q, w_query, preferred_element_type=jnp.float32).astype(jnp.bfloat16)
        key_proj = jnp.dot(source_kv, w_key, preferred_element_type=jnp.float32).astype(
            jnp.bfloat16
        )
        value_proj = jnp.dot(source_kv, w_value, preferred_element_type=jnp.float32).astype(
            jnp.bfloat16
        )
        query, key_proj, value_proj = (
            lax.all_to_all(query, "ffn", split_axis=1, concat_axis=0, tiled=True),
            lax.all_to_all(key_proj, "ffn", split_axis=1, concat_axis=0, tiled=True),
            lax.all_to_all(value_proj, "ffn", split_axis=1, concat_axis=0, tiled=True),
        )
        mixed, log_totals = attend(query, key_proj, value_proj, live_of, table_part, causal)
        merged = lax.all_to_all(mixed, "ffn", split_axis=0, concat_axis=1, tiled=True)
        branch = jnp.dot(merged, w_out, preferred_element_type=jnp.float32)
        return (
            branch,
            (query, key_proj, value_proj, mixed, log_totals, merged, source_q, source_kv),
        )

    def attention_backward(
        layer_index, grad_branch, stored, shared_source, live_of, table_part, causal
    ):
        query, key_proj, value_proj, mixed, log_totals, merged, source_q, source_kv = stored
        w_query = qk_weights[layer_index, 0]
        w_key = qk_weights[layer_index, 1]
        w_value = v_weights[layer_index]
        w_out = out_weights[layer_index]
        grad_low = grad_branch.astype(jnp.bfloat16)
        grad_merged = product(grad_low, w_out, contract_last).astype(jnp.bfloat16)
        grad_mixed = lax.all_to_all(grad_merged, "ffn", split_axis=1, concat_axis=0, tiled=True)
        head_query, head_keys, head_values, grad_table = attend_back(
            query, key_proj, value_proj, log_totals, grad_mixed, live_of, table_part, causal
        )
        grad_query, grad_keys, grad_values = (
            lax.all_to_all(head_query, "ffn", split_axis=0, concat_axis=1, tiled=True),
            lax.all_to_all(head_keys, "ffn", split_axis=0, concat_axis=1, tiled=True),
            lax.all_to_all(head_values, "ffn", split_axis=0, concat_axis=1, tiled=True),
        )
        from_query = product(grad_query, w_query, contract_last)
        from_memory = product(grad_keys, w_key, contract_last) + product(
            grad_values, w_value, contract_last
        )
        if shared_source:
            from_query = from_query + from_memory
        weight_terms = (
            product(source_q, grad_query, contract_rows),
            product(source_kv, grad_keys, contract_rows),
            product(source_kv, grad_values, contract_rows),
            product(merged, grad_low, contract_rows),
        )
        return (from_query, from_memory, weight_terms, grad_table)

    def ffn_forward(layer_index, normed):
        gathered = ffn_rows(normed)
        pre = jnp.dot(gathered, ffn_in[layer_index], preferred_element_type=jnp.float32)
        hidden = gelu_exact(pre).astype(jnp.bfloat16)
        branch = ffn_sum(hidden, ffn_out[layer_index], contract_plain)
        return (branch, (gathered, pre, hidden))

    def ffn_backward(layer_index, grad_branch, stored):
        gathered, pre, hidden = stored
        grad_rows = ffn_rows(grad_branch.astype(jnp.bfloat16))
        grad_hidden = product(grad_rows, ffn_out[layer_index], contract_last).astype(jnp.bfloat16)
        grad_pre = (grad_hidden.astype(jnp.float32) * gelu_slope(pre)).astype(jnp.bfloat16)
        grad_down = product(hidden, grad_rows, contract_rows)
        grad_up = product(gathered, grad_pre, contract_rows)
        from_input = ffn_sum(grad_pre, ffn_in[layer_index], contract_last)
        return (from_input, grad_up, grad_down)

    enc_start = enc_in.astype(jnp.float32)
    normed_a = rms_scale(enc_start, gains[0]).astype(jnp.bfloat16)
    branch_a, stored_a = attention_forward(0, normed_a, normed_a, enc_live, enc_table, False)
    enc_mid = enc_start + branch_a
    normed_b = rms_scale(enc_mid, gains[1]).astype(jnp.bfloat16)
    branch_b, stored_b = ffn_forward(0, normed_b)
    enc_last = enc_mid + branch_b
    memory = rms_scale(enc_last, gains[2]).astype(jnp.bfloat16)
    dec_start = dec_in.astype(jnp.float32)
    normed_c = rms_scale(dec_start, gains[3]).astype(jnp.bfloat16)
    branch_c, stored_c = attention_forward(1, normed_c, normed_c, self_live, dec_table, True)
    dec_first = dec_start + branch_c
    normed_d = rms_scale(dec_first, gains[4]).astype(jnp.bfloat16)
    branch_d, stored_d = attention_forward(2, normed_d, memory, cross_live, None, False)
    dec_second = dec_first + branch_d
    normed_e = rms_scale(dec_second, gains[5]).astype(jnp.bfloat16)
    branch_e, stored_e = ffn_forward(1, normed_e)
    dec_final = dec_second + branch_e
    grad_final = cotangent.astype(jnp.float32)
    from_ffn_dec, up_dec, down_dec = ffn_backward(1, grad_final, stored_e)
    grad_norm_in, gain_e = norm_back(dec_second, gains[5], from_ffn_dec)
    grad_second = grad_final + grad_norm_in
    from_cross, to_memory, cross_weights, unused_table = attention_backward(
        2, grad_second, stored_d, False, cross_live, None, False
    )
    grad_norm_in, gain_d = norm_back(dec_first, gains[4], from_cross)
    grad_first = grad_second + grad_norm_in
    from_self, unused_memory, self_weights, dec_table_grad = attention_backward(
        1, grad_first, stored_c, True, self_live, dec_table, True
    )
    grad_norm_in, gain_c = norm_back(dec_start, gains[3], from_self)
    dec_total = grad_first + grad_norm_in
    grad_last, gain_memory = norm_back(enc_last, gains[2], to_memory)
    from_ffn_enc, up_enc, down_enc = ffn_backward(0, grad_last, stored_b)
    grad_norm_in, gain_b = norm_back(enc_mid, gains[1], from_ffn_enc)
    grad_mid = grad_last + grad_norm_in
    from_enc, unused_source, enc_weights, enc_table_grad = attention_backward(
        0, grad_mid, stored_a, True, enc_live, enc_table, False
    )
    grad_norm_in, gain_a = norm_back(enc_start, gains[0], from_enc)
    enc_total = grad_mid + grad_norm_in
    qk_full = jnp.stack(
        [
            jnp.stack([enc_weights[0], enc_weights[1]]),
            jnp.stack([self_weights[0], self_weights[1]]),
            jnp.stack([cross_weights[0], cross_weights[1]]),
        ]
    )
    value_full = jnp.stack([enc_weights[2], self_weights[2], cross_weights[2]])
    out_full = jnp.stack([enc_weights[3], self_weights[3], cross_weights[3]])
    up_full = jnp.stack([up_enc, up_dec])
    down_full = jnp.stack([down_enc, down_dec])
    row_share = model_width // token_groups
    qk_order = (
        qk_full.reshape(3, 2, token_groups, row_share, group_size, local_width)
        .transpose(0, 1, 2, 4, 3, 5)
        .reshape(3, 2, token_groups * group_size * row_share, local_width)
    )
    value_order = (
        value_full.reshape(3, token_groups, row_share, group_size, local_width)
        .transpose(0, 1, 3, 2, 4)
        .reshape(3, token_groups * group_size * row_share, local_width)
    )
    out_order = (
        out_full.reshape(3, group_size, local_width, token_groups, row_share)
        .transpose(0, 3, 1, 2, 4)
        .reshape(3, token_groups * group_size * local_width, row_share)
    )
    qk_grad, value_grad, out_grad = (
        lax.psum_scatter(qk_order, ("tok", "ffn"), scatter_dimension=2, tiled=True),
        lax.psum_scatter(value_order, ("tok", "ffn"), scatter_dimension=1, tiled=True),
        lax.psum_scatter(out_order, ("tok", "ffn"), scatter_dimension=1, tiled=True),
    )
    up_grad, down_grad = (
        lax.psum_scatter(up_full, "tok", scatter_dimension=1, tiled=True),
        lax.psum_scatter(down_full, "tok", scatter_dimension=2, tiled=True),
    )
    table_terms = jnp.zeros((2, BUCKETS, bias_tables.shape[2]), jnp.float32)
    table_terms = lax.dynamic_update_slice(
        table_terms,
        jnp.stack([enc_table_grad, dec_table_grad]),
        (jnp.int32(0), jnp.int32(0), group_index * local_heads),
    )
    gain_terms = jnp.stack([gain_a, gain_b, gain_memory, gain_c, gain_d, gain_e])
    gain_grad, table_grad = lax.psum((gain_terms, table_terms), ("tok", "ffn"))
    return (
        dec_final.astype(jnp.bfloat16),
        enc_total.astype(jnp.bfloat16),
        dec_total.astype(jnp.bfloat16),
        qk_grad,
        value_grad,
        out_grad,
        up_grad,
        down_grad,
        table_grad,
        gain_grad,
        gain_grad[5],
    )


def solution(mesh):
    placed = (
        P(("tok", "ffn"), None),
        P(("tok", "ffn"), None),
        P(("tok", "ffn"), None),
        P("tok", None),
        P("tok", None),
        P(),
        P(),
        P(),
        P(None, None, "ffn"),
        P(None, "ffn", None),
        P(),
        P(),
    )
    return jax.shard_map(
        on_device,
        mesh=mesh,
        in_specs=placed,
        out_specs=(
            P(("tok", "ffn"), None),
            P(("tok", "ffn"), None),
            P(("tok", "ffn"), None),
            P(None, None, "tok", "ffn"),
            P(None, "tok", "ffn"),
            P(None, "ffn", "tok"),
            P(None, "tok", "ffn"),
            P(None, "ffn", "tok"),
            P(),
            P(),
            P(),
        ),
        check_vma=False,
    )
```

profile of v0, /device:TPU:0, one launch (start us, length us, event | category | flops | bytes accessed | tf_op | source)
XLA Modules:
  0.0 1292.7 jit_solution(5401394682397760932)
XLA Ops:
  34.3 18.8 %copy.379 = f32[1,3,640,1280]{3,1,2,0:T(4,128)S(1)} copy(f32[1,3,640,1280]{3,2,1,0:T(8,128)} %broadcast_bitcast_fusion) | data formatting | bytes 19660800
  53.1 5.3 slice.164
  58.4 13.6 %reshape.852 = f32[2455680]{0:T(1024)} reshape(f32[3,818560]{1,0:T(4,128)} %slice.164) | data formatting | bytes 19645440
  72.1 19.4 %reshape.777 = f32[3,640,1279]{2,1,0:T(8,128)} reshape(f32[2455680]{0:T(1024)} %reshape.852) | data formatting | bytes 19645440 | tf_op jit(solution)/shard_map/while/body/eval_jaxpr/reshape | solution.py:69
  91.5 6.4 slice.165
  98.0 7.0 copy.375
  108.2 19.2 %copy.378 = f32[1,3,640,1280]{3,1,2,0:T(4,128)S(1)} copy(f32[1,3,640,1280]{3,2,1,0:T(8,128)} %broadcast_bitcast_fusion.1) | data formatting | bytes 19660800
  127.4 5.1 slice.162
  132.5 13.6 %reshape.850 = f32[2455680]{0:T(1024)} reshape(f32[3,818560]{1,0:T(4,128)} %slice.162) | data formatting | bytes 19645440
  146.2 19.4 %reshape.772 = f32[3,640,1279]{2,1,0:T(8,128)} reshape(f32[2455680]{0:T(1024)} %reshape.850) | data formatting | bytes 19645440 | tf_op jit(solution)/shard_map/while/body/eval_jaxpr/reshape | solution.py:69
  165.5 6.5 slice.163
  172.0 7.0 copy.374
  183.7 6.7 all-to-all-done.6
  196.3 4.5 all-to-all-done.4
  204.3 5.7 fusion.255
  234.8 5.7 fusion.254
  244.3 10.1 all_gather.12
  254.5 6.6 multiply_convert_fusion.6
  271.1 9.2 all_to_all.420
  310.7 5.6 all-to-all-done.8
  326.5 13.3 %all_gather.14 = bf16[640,768]{1,0:T(8,128)(2,1)} all-gather(bf16[160,768]{1,0:T(8,128)(2,1)S(1)} %copy-done.44), channel_id=1, replica_groups=mesh['tok'=8,'ffn'=4] {'ffn'}, dimensions={0}, use_global_device_ids=true | all-gather | bytes 1228800 | tf_op jit(solution)/shard_map/all_gather | solution.py:228
  342.3 9.8 all_gather.13
  352.1 11.9 multiply_convert_fusion.5
  372.3 21.7 %reduce-scatter.15.cloned.1.call-done = bf16[160,768]{1,0:T(8,128)(2,1)} async-done(((bf16[640,768]{1,0:T(8,128)(2,1)}), bf16[160,768]{1,0:T(8,128)(2,1)}) %reduce-scatter.15.cloned.1.call-update) | async-done | bytes 245776 | tf_op jit(solution)/shard_map/reduce_scatter | solution.py:231
  395.7 25.4 %reduce-scatter.13.cloned.1.call-done = bf16[160,768]{1,0:T(8,128)(2,1)} async-done(((bf16[640,768]{1,0:T(8,128)(2,1)}), bf16[160,768]{1,0:T(8,128)(2,1)}) %reduce-scatter.13.cloned.1.call-update) | async-done | bytes 245776 | tf_op jit(solution)/shard_map/reduce_scatter | solution.py:231
  429.5 6.7 all-to-all-done.12
  439.2 6.5 multiply_reduce_fusion.2
  453.7 5.2 multiply_convert_fusion.2
  478.4 9.1 all_gather.15
  498.1 8.3 copy.313
  543.4 14.5 %copy.369 = f32[3,8,4,192,96]{4,0,3,2,1:T(4,128)} copy(f32[3,8,4,192,96]{4,3,1,2,0:T(8,128)S(1)} %maximum_bitcast_fusion) | data formatting | bytes 14155776
  557.9 15.9 %reshape.838 = f32[6144,288]{1,0:T(8,128)} reshape(f32[6144,3,96]{2,1,0:T(4,128)} %bitcast.453) | data formatting | bytes 14155776
  625.7 4.5 all-to-all-start.21
  640.8 5.6 pad.22.clone
  646.4 11.0 reshape.854
  657.4 10.8 reshape.801
  684.9 6.7 all-to-all-done.15
  750.9 6.7 pad_maximum_fusion
  757.6 5.4 pad_convert_fusion
  776.7 5.6 pad.20.clone
  782.3 11.1 reshape.856
  793.4 10.9 reshape.798
  812.1 8.2 maximum_maximum_fusion
  820.3 5.0 pad_convert_fusion.1
  827.2 43.2 %all-reduce.5 = (f32[2,32,12]{1,0,2:T(2,128)}, f32[6,768]{1,0:T(8,128)S(1)}) all-reduce(f32[2,32,12]{1,0,2:T(2,128)S(1)} %copy_dynamic-update-slice_fusion, f32[6,768]{1,0:T(8,128)S(1)} %stack.84), channel_id=1, replica_groups=mesh['tok'=8,'ffn'=4] {'tok','ffn'}, use_global_device_ids=true, to_apply=%region_39.40 | all-reduce | flops 5376 | bytes 43008 | tf_op jit(solution)/shard_map/psum | solution.py:397
  875.0 55.5 %reduce-scatter.23.cloned.1.call-done = f32[2,96,768]{2,1,0:T(8,128)} async-done(((f32[2,768,768]{2,1,0:T(8,128)}), f32[2,96,768]{2,1,0:T(8,128)}) %reduce-scatter.23.cloned.1.call-update) | async-done | bytes 589840 | tf_op jit(solution)/shard_map/reduce_scatter | solution.py:387
  930.5 142.6 %reduce-scatter.21.cloned.1.call-done = f32[3,96,192]{2,1,0:T(8,128)} async-done(((f32[3,3072,192]{2,1,0:T(8,128)}), f32[3,96,192]{2,1,0:T(8,128)}) %reduce-scatter.21.cloned.1.call-update) | async-done | bytes 221200 | tf_op jit(solution)/shard_map/reduce_scatter | solution.py:383
  1073.1 212.9 %reduce-scatter.19.cloned.1.call-done = f32[3,2,96,192]{3,2,1,0:T(8,128)} async-done(((f32[3,2,3072,192]{3,2,1,0:T(8,128)}), f32[3,2,96,192]{3,2,1,0:T(8,128)}) %reduce-scatter.19.cloned.1.call-update) | async-done | bytes 442384 | tf_op jit(solution)/shard_map/reduce_scatter | solution.py:382
  (604 shorter events, 385.7 us)
Async XLA Ops:
  8.2 14.1 %copy-start.89 = (f32[768]{0:T(1024)}, f32[768]{0:T(1024)S(1)}, u32[]{:S(2)}) copy-start(f32[768]{0:T(1024)S(1)} %get-tuple-element.272) | copy-start | bytes 9220
  8.2 274.6 %copy-start.91 = (f32[768]{0:T(1024)}, f32[768]{0:T(1024)S(1)}, u32[]{:S(2)}) copy-start(f32[768]{0:T(1024)S(1)} %get-tuple-element.273) | copy-start | bytes 9220
  12.3 168.0 %all-to-all-start.5 = ((bf16[160,4,192]{2,0,1:T(8,128)(2,1)}), bf16[160,4,192]{2,0,1:T(8,128)(2,1)S(1)}, u32[]{:S(2)}, u32[]{:S(2)}) async-start(bf16[160,4,192]{2,0,1:T(8,128)(2,1)} %copy.238), calls=%async_computation.5 | async-start | bytes 655360 | tf_op jit(solution)/shard_map/all_to_all | solution.py:251
  180.2 10.2 all-to-all-start.6
  190.4 10.4 all-to-all-start.4
  195.2 14.7 %copy-start.7 = (pred[640,640]{0,1:T(8,128)(4,1)}, pred[640,640]{0,1:T(8,128)(4,1)S(1)}, u32[]{:S(2)}) copy-start(pred[640,640]{0,1:T(8,128)(4,1)S(1)} %get-tuple-element.295) | copy-start | bytes 1228804
  195.2 409.8 %copy-start.10 = (pred[640,640]{0,1:T(8,128)(4,1)}, pred[640,640]{0,1:T(8,128)(4,1)S(1)}, u32[]{:S(2)}) copy-start(pred[640,640]{0,1:T(8,128)(4,1)S(1)} %get-tuple-element.296) | copy-start | bytes 1228804
  195.8 14.2 %copy-start.21 = (bf16[640,3,64]{0,2,1:T(8,128)(2,1)}, bf16[640,3,64]{0,2,1:T(8,128)(2,1)S(1)}, u32[]{:S(2)}) copy-start(bf16[640,3,64]{0,2,1:T(8,128)(2,1)S(1)} %reshape.774) | copy-start | bytes 737284
  200.8 10.2 all-to-all-start.1
  210.0 14.6 %copy-start.72 = (f32[3,640]{1,0:T(4,128)}, f32[3,640]{1,0:T(4,128)S(1)}, u32[]{:S(2)}) copy-start(f32[3,640]{1,0:T(4,128)S(1)} %get-tuple-element.299) | copy-start | bytes 23044
  210.5 14.1 %copy-start.57 = (bf16[640,3,64]{0,2,1:T(8,128)(2,1)}, bf16[640,3,64]{0,2,1:T(8,128)(2,1)S(1)}, u32[]{:S(2)}) copy-start(bf16[640,3,64]{0,2,1:T(8,128)(2,1)S(1)} %reshape.773) | copy-start | bytes 737284
  211.0 10.2 all-to-all-start.2
  221.1 10.2 all-to-all-start
  231.3 10.4 all-to-all-start.7
  234.8 55.7 %reduce-scatter.11.cloned.1.call-start = ((), (), s32[]{:S(2)}) async-start(), calls=%async_computation.32 | async-start | bytes 1228800 | tf_op jit(solution)/shard_map/reduce_scatter | solution.py:231
  240.5 26.6 %copy-start.74 = (f32[3,640]{1,0:T(4,128)}, f32[3,640]{1,0:T(4,128)S(1)}, u32[]{:S(2)}) copy-start(f32[3,640]{1,0:T(4,128)S(1)} %get-tuple-element.297) | copy-start | bytes 23044
  242.3 18.8 %copy-start.63 = (bf16[160,768]{1,0:T(8,128)(2,1)}, bf16[160,768]{1,0:T(8,128)(2,1)S(1)}, u32[]{:S(2)}) copy-start(bf16[160,768]{1,0:T(8,128)(2,1)S(1)} %all_to_all.337) | copy-start | bytes 737284
  244.2 16.8 %copy-start.108 = (f32[160]{0:T(256)}, f32[160]{0:T(256)S(1)}, u32[]{:S(2)}) copy-start(f32[160]{0:T(256)S(1)} %get-tuple-element.301) | copy-start | bytes 1924
  244.2 16.8 %copy-start.82 = (f32[160]{0:T(256)}, f32[160]{0:T(256)S(1)}, u32[]{:S(2)}) copy-start(f32[160]{0:T(256)S(1)} %fusion.230) | copy-start | bytes 1924
  282.7 57.5 %copy-start.38 = (f32[160,768]{1,0:T(8,128)}, f32[160,768]{1,0:T(8,128)S(1)}, u32[]{:S(2)}) copy-start(f32[160,768]{1,0:T(8,128)S(1)} %get-tuple-element.305) | copy-start | bytes 1474564
  285.7 10.2 all-to-all-start.9
  295.9 10.2 all-to-all-start.10
  306.0 10.3 all-to-all-start.8
  322.9 16.8 %all-to-all-start.11 = ((bf16[4,160,192]{2,1,0:T(8,128)(2,1)}), bf16[4,160,192]{2,1,0:T(8,128)(2,1)S(1)}, u32[]{:S(2)}, u32[]{:S(2)}) async-start(bf16[4,160,192]{2,1,0:T(8,128)(2,1)} %copy.253), calls=%async_computation.12 | async-start | bytes 655360 | tf_op jit(solution)/shard_map/all_to_all | solution.py:256
  326.4 67.6 %reduce-scatter.15.cloned.1.call-start = ((), (), s32[]{:S(2)}) async-start(), calls=%async_computation.34 | async-start | bytes 1228800 | tf_op jit(solution)/shard_map/reduce_scatter | solution.py:231
  368.3 52.9 %reduce-scatter.13.cloned.1.call-start = ((), (), s32[]{:S(2)}) async-start(), calls=%async_computation.33 | async-start | bytes 1228800 | tf_op jit(solution)/shard_map/reduce_scatter | solution.py:231
  426.1 10.2 all-to-all-start.12
  450.2 12.4 all-to-all-start.14
  462.6 10.3 all-to-all-start.13
  466.2 67.2 %reduce-scatter.17.cloned.1.call-start = ((), (), s32[]{:S(2)}) async-start(), calls=%async_computation.35 | async-start | bytes 1228800 | tf_op jit(solution)/shard_map/reduce_scatter | solution.py:231
  473.5 14.0 %copy-start.135 = (f32[640,768]{1,0:T(8,128)S(1)}, f32[640,768]{1,0:T(8,128)}, u32[]{:S(2)}) copy-start(f32[640,768]{1,0:T(8,128)} %get-tuple-element.303) | copy-start | bytes 5898244
  491.6 379.4 %all-reduce.8.cloned.1.call-start = ((), (), s32[]{:S(2)}) async-start(), calls=%async_computation.40 | async-start | bytes 9437184
  512.7 11.5 all-to-all-start.19
  516.2 356.9 %reduce-scatter.25.cloned.1.call-start = ((), (), s32[]{:S(2)}) async-start(), calls=%async_computation.39 | async-start | bytes 9732096
  573.8 356.6 %reduce-scatter.23.cloned.1.call-start = ((), (), s32[]{:S(2)}) async-start(), calls=%async_computation.38 | async-start | bytes 5308416 | tf_op jit(solution)/shard_map/reduce_scatter | solution.py:387
  582.1 23.0 %copy-start.77 = (f32[3,640]{1,0:T(4,128)}, f32[3,640]{1,0:T(4,128)S(1)}, u32[]{:S(2)}) copy-start(f32[3,640]{1,0:T(4,128)S(1)} %log_add_fusion) | copy-start | bytes 23044
  585.0 10.4 all-to-all-start.20
  600.8 14.8 %all-to-all-start.23 = ((bf16[4,160,192]{2,1,0:T(8,128)(2,1)}), bf16[4,160,192]{2,1,0:T(8,128)(2,1)}, u32[]{:S(2)}, u32[]{:S(2)}) async-start(bf16[4,160,192]{2,1,0:T(8,128)(2,1)} %copy.286), calls=%async_computation.27 | async-start | bytes 655360 | tf_op jit(solution)/shard_map/all_to_all | solution.py:280
  615.6 10.2 all-to-all-start.22
  625.7 44.6 %all-to-all-start.21 = ((bf16[4,160,192]{2,1,0:T(8,128)(2,1)}), bf16[4,160,192]{2,1,0:T(8,128)(2,1)}, u32[]{:S(2)}, u32[]{:S(2)}) async-start(bf16[4,160,192]{2,1,0:T(8,128)(2,1)} %copy.280), calls=%async_computation.25 | async-start | bytes 655360 | tf_op jit(solution)/shard_map/all_to_all | solution.py:278
  681.5 10.2 all-to-all-start.15
  697.0 12.5 all-to-all-start.18
  709.4 10.9 all-to-all-start.17
  720.3 15.2 %all-to-all-start.16 = ((bf16[4,160,192]{2,1,0:T(8,128)(2,1)}), bf16[4,160,192]{2,1,0:T(8,128)(2,1)}, u32[]{:S(2)}, u32[]{:S(2)}) async-start(bf16[4,160,192]{2,1,0:T(8,128)(2,1)} %copy.266), calls=%async_computation.20 | async-start | bytes 655360 | tf_op jit(solution)/shard_map/all_to_all | solution.py:278
  724.5 348.6 %reduce-scatter.21.cloned.1.call-start = ((), (), s32[]{:S(2)}) async-start(), calls=%async_computation.37 | async-start | bytes 9732096 | tf_op jit(solution)/shard_map/reduce_scatter | solution.py:383
  757.6 528.4 %reduce-scatter.19.cloned.1.call-start = ((), (), s32[]{:S(2)}) async-start(), calls=%async_computation.36 | async-start | bytes 19464192 | tf_op jit(solution)/shard_map/reduce_scatter | solution.py:382
  793.4 17.3 %copy-start.6 = (f32[1,1,8,96,4,192]{5,3,4,2,1,0:T(8,128)S(1)}, f32[1,1,8,96,4,192]{5,3,4,2,1,0:T(8,128)}, u32[]{:S(2)}) copy-start(f32[1,1,8,96,4,192]{5,3,4,2,1,0:T(8,128)} %convolution_bitcast_fusion.9) | copy-start | bytes 7077892
  870.4 415.6 %copy-start.119 = (f32[6,768]{1,0:T(8,128)}, f32[6,768]{1,0:T(8,128)S(1)}, u32[]{:S(2)}) copy-start(f32[6,768]{1,0:T(8,128)S(1)} %get-tuple-element.275) | copy-start | bytes 55300
  (126 other events, 740.3 us)
Sparse Core Ops, SparseCore 0:
  264.1 26.3 reduce-scatter.10
  368.4 25.5 reduce-scatter.14
  396.6 24.5 reduce-scatter.12
  491.7 25.0 reduce-scatter.16
  520.3 169.6 all-reduce.7
  695.8 134.6 reduce-scatter.24
  835.1 95.2 reduce-scatter.22
  937.9 135.0 reduce-scatter.20
  1080.0 205.9 reduce-scatter.18
where the time goes:
time: 1300 us; the launch traced here: 1290 us
  waiting for transfers between devices  510 us (39%)
  local copies, waits for them, and re-layouts  353 us (27%)
  matrix products  163 us (13%)
  blocking collectives  94.7 us (7%)
  starting transfers between devices  86 us (7%)
  other arithmetic  69 us (5%)
  between operations  17.3 us (1%)
    reduce_scatter x1, waiting for transfers between devices, on_device(): lax.psum_scatter(qk_order, ('tok', 'ffn'), scatter_dimension=2, tiled=True)  213 us
    unnamed x303, local copies, waits for them, and re-layouts  163 us
    reduce_scatter x1, waiting for transfers between devices, on_device(): lax.psum_scatter(value_order, ('tok', 'ffn'), scatter_dimension=1, tiled=...  143 us
    dot_general x34, matrix products, product(): lax.dot_general(left, right, contract, preferred_element_type=jnp.float32)  70.5 us
    reshape x4, local copies, waits for them, and re-layouts, bias_block(): spread[:, :block_rows * (line_width - 1)]  60.5 us
    reduce_scatter x1, waiting for transfers between devices, on_device(): lax.psum_scatter(up_full, 'tok', scatter_dimension=1, tiled=True)  55.5 us
    reduce_scatter x4, waiting for transfers between devices, ffn_sum(): lax.psum_scatter(product(left, right, contract).astype(jnp.bfloat16), 'ff...  48.5 us
    psum x1, blocking collectives, on_device(): gain_grad, table_grad = lax.psum((gain_terms, table_terms), ('tok', 'ffn'))  43.2 us
  transfers between devices with their start and end apart: 32, of which 20 were waited for; matrix products, arithmetic and copies ran while one was open for 38% of the time, Pallas kernels for 0%

commit v1 on v0

v1 whole, which is shorter than its diff:
```python
import functools
import jax
import jax.numpy as jnp
from jax import lax
from jax.experimental import pallas as pl
from jax.experimental.pallas import tpu as pltpu
from jax.sharding import PartitionSpec as P

DH = 64
BUCKETS = 32
SLOT = 128
GROUP = 4
BF = jnp.bfloat16
F32 = jnp.float32
MESH = pl.DeviceIdType.MESH

norm_epsilon = 1e-06
masked_score = -1000000000.0
wide_limits = (1, 2, 3, 4, 5, 6, 7, 8, 12, 16, 23, 32, 46, 64, 91)
causal_limits = tuple(range(1, 16)) + (
    16, 19, 21, 24, 27, 31, 35, 40, 46, 52, 59, 67, 77, 87, 99, 113,
)


def nn(a, b):
    return lax.dot_general(a, b, (((1,), (0,)), ((), ())), preferred_element_type=F32)


def nt(a, b):
    return lax.dot_general(a, b, (((1,), (1,)), ((), ())), preferred_element_type=F32)


def tn(a, b):
    return lax.dot_general(a, b, (((0,), (0,)), ((), ())), preferred_element_type=F32)


def iota(shape, axis):
    return lax.broadcasted_iota(jnp.int32, shape, axis)


def rms(v, gain):
    return v * lax.rsqrt(jnp.mean(v * v, axis=-1, keepdims=True) + norm_epsilon) * gain


def rms_back(v, gain, e):
    s = lax.rsqrt(jnp.mean(v * v, axis=-1, keepdims=True) + norm_epsilon)
    eg = e * gain
    vs = v * s
    grad = s * (eg - vs * (s * jnp.mean(eg * v, axis=-1, keepdims=True)))
    return grad, jnp.sum(e * vs, axis=0, keepdims=True)


def gelu_cdf(x):
    return 0.5 * (1.0 + lax.erf(x * 0.7071067811865476))


def gelu_slope(x, cdf):
    return cdf + x * (0.3989422804014327 * jnp.exp(-0.5 * x * x))


class Refs:
    pass


class Group:
    def __init__(self, r, rows):
        self.r = r
        self.rows = rows
        self.t = lax.axis_index("tok")
        self.f = lax.axis_index("ffn")
        self.c = self.f % 2
        self.sib = self.f + 1 - 2 * self.c
        self.cross = (self.f + 2) % GROUP
        self.diag = (self.sib + 2) % GROUP
        self.near = (self.f // 2) * (2 * rows)
        self.far = 2 * rows - self.near
        self.count = 0

    def slot(self, index):
        return pl.ds(pl.multiple_of(index * self.rows, 16), self.rows)

    def near_rows(self):
        return pl.ds(pl.multiple_of(self.near, 16), 2 * self.rows)

    def far_rows(self):
        return pl.ds(pl.multiple_of(self.far, 16), 2 * self.rows)

    def signal(self):
        barrier = pltpu.get_barrier_semaphore()
        for other in (self.sib, self.cross, self.diag):
            pl.semaphore_signal(barrier, inc=1, device_id=(self.t, other), device_id_type=MESH)

    def wait(self):
        pl.semaphore_wait(pltpu.get_barrier_semaphore(), 3)

    def copy(self, src, dst, other):
        k = self.count
        self.count += 1
        return pltpu.make_async_remote_copy(
            src_ref=src,
            dst_ref=dst,
            send_sem=self.r.send.at[k],
            recv_sem=self.r.recv.at[k],
            device_id=(self.t, other),
            device_id_type=MESH,
        )


class Gather:
    def __init__(self, g, ref):
        self.g, self.ref = g, ref
        own = ref.at[g.slot(g.f), :]
        self.x = g.copy(own, own, g.cross)
        self.s = g.copy(own, own, g.sib)
        got = ref.at[g.slot(g.cross), :]
        self.h = g.copy(got, got, g.sib)

    def start(self):
        self.x.start()
        self.s.start()

    def near(self):
        self.s.wait_recv()

    def relay(self):
        self.x.wait_recv()
        self.h.start()

    def far(self):
        self.h.wait_recv()

    def done(self):
        self.x.wait_send()
        self.s.wait_send()
        self.h.wait_send()


class Scatter:
    def __init__(self, g, near_f32, far_low, sib_low, sum_low, got):
        self.g = g
        self.near_f32, self.far_low, self.sib_low, self.sum_low, self.got = (
            near_f32, far_low, sib_low, sum_low, got,
        )
        self.a = g.copy(far_low.at[1 - g.c], got.at[0], g.sib)
        self.b = g.copy(sib_low, got.at[1], g.sib)
        self.x = g.copy(sum_low, got.at[2], g.cross)

    def put_far(self, value):
        rows = self.g.rows
        low = value.astype(BF)
        self.far_low[0] = low[:rows]
        self.far_low[1] = low[rows:]
        self.a.start()

    def put_near(self, value):
        rows = self.g.rows
        self.near_f32[0] = value[:rows]
        self.near_f32[1] = value[rows:]
        self.sib_low[...] = self.near_f32[1 - self.g.c].astype(BF)
        self.b.start()

    def relay(self):
        self.a.wait_recv()
        total = self.got[0].astype(F32) + self.far_low[self.g.c].astype(F32)
        self.sum_low[...] = total.astype(BF)
        self.x.start()

    def result(self):
        self.b.wait_recv()
        part = self.near_f32[self.g.c] + self.got[1].astype(F32)
        self.x.wait_recv()
        return part + self.got[2].astype(F32)

    def done(self):
        self.a.wait_send()
        self.b.wait_send()
        self.x.wait_send()


def scatter_scratch(tag, rows, width):
    return {
        tag + "_near": ((2, rows, width), F32),
        tag + "_far": ((2, rows, width), BF),
        tag + "_sib": ((rows, width), BF),
        tag + "_sum": ((rows, width), BF),
        tag + "_got": ((3, rows, width), BF),
    }


def scatter_of(g, r, tag):
    return Scatter(
        g,
        getattr(r, tag + "_near"),
        getattr(r, tag + "_far"),
        getattr(r, tag + "_sib"),
        getattr(r, tag + "_sum"),
        getattr(r, tag + "_got"),
    )


class Exchange:
    def __init__(self, g, src, dst):
        self.g, self.src, self.dst = g, src, dst
        self.copies = [
            g.copy(src.at[g.slot(other), :], dst.at[g.f], other)
            for other in (g.diag, g.cross, g.sib)
        ]

    def start(self):
        for copy in self.copies:
            copy.start()
        self.dst[self.g.f] = self.src[self.g.slot(self.g.f), :]

    def recv(self):
        for copy in self.copies:
            copy.wait_recv()

    def done(self):
        for copy in self.copies:
            copy.wait_send()


def merged_out(dst, w_out):
    width = dst.shape[2]
    total = nn(dst[0], w_out[:width, :])
    for p in range(1, GROUP):
        total = total + nn(dst[p], w_out[p * width : (p + 1) * width, :])
    return total


def run(name, cid, body, ins, outs, scratch, copies, rows):
    in_names, out_names, scr_names = list(ins), list(outs), list(scratch)

    def kernel(*refs):
        r = Refs()
        for n, ref in zip(in_names + out_names + scr_names + ["send", "recv"], refs):
            setattr(r, n, ref)
        body(r, Group(r, rows))

    spaces = {"v": pltpu.VMEM, "s": pltpu.SMEM}
    got = pl.pallas_call(
        kernel,
        out_shape=[jax.ShapeDtypeStruct(*outs[n]) for n in out_names],
        in_specs=[pl.BlockSpec(memory_space=spaces[ins[n][1]]) for n in in_names],
        out_specs=[pl.BlockSpec(memory_space=pltpu.VMEM) for n in out_names],
        scratch_shapes=[pltpu.VMEM(*scratch[n]) for n in scr_names]
        + [pltpu.SemaphoreType.DMA((copies,)), pltpu.SemaphoreType.DMA((copies,))],
        compiler_params=pltpu.CompilerParams(
            collective_id=cid, has_side_effects=True, vmem_limit_bytes=62 * 2**20
        ),
        name=name,
    )(*[ins[n][0] for n in in_names])
    return dict(zip(out_names, got))


def enc_starts(lens, count):
    starts = [jnp.int32(0)]
    for e in range(count):
        starts.append(starts[-1] + lens[0, e])
    return starts


def segment_of(place, starts):
    total = jnp.zeros(place.shape, jnp.int32)
    for s in starts[1:-1]:
        total = total + (place >= s).astype(jnp.int32)
    return total


def enc_bias_blocks(tables, out, f, heads, blocks):
    side = SLOT
    r = iota((side, side), 1) - iota((side, side), 0)
    for d in range(-(blocks - 1), blocks):
        far = blocks - 1 + d
        if abs(d) >= 2:
            for h in range(heads):
                value = tables[0, 31 if d > 0 else 15, f * heads + h]
                out[h, far] = jnp.full((side, side), value, F32)
            continue
        rel = r + d * side
        values = [jnp.full((side, side), tables[0, 0 if d <= 0 else 17, f * heads + h], F32) for h in range(heads)]
        if d >= 0:
            for b, limit in enumerate(wide_limits):
                hit = rel >= limit
                values = [
                    jnp.where(hit, tables[0, 17 + b, f * heads + h], values[h]) for h in range(heads)
                ]
        if d <= 0:
            for b, limit in enumerate(wide_limits):
                hit = rel <= -limit
                values = [
                    jnp.where(hit, tables[0, 1 + b, f * heads + h], values[h]) for h in range(heads)
                ]
        for h in range(heads):
            out[h, far] = values[h]


def dec_bias_block(tables, out, f, heads):
    side = SLOT
    m = iota((side, side), 0) - iota((side, side), 1)
    values = [jnp.full((side, side), tables[1, 0, f * heads + h], F32) for h in range(heads)]
    for b, limit in enumerate(causal_limits):
        hit = m >= limit
        values = [jnp.where(hit, tables[1, 1 + b, f * heads + h], values[h]) for h in range(heads)]
    for h in range(heads):
        out[h] = values[h]


def put_heads(ref, rows, value, first):
    low = value.astype(BF)
    for j in range(low.shape[1] // DH):
        ref[first + j, rows, :] = low[:, j * DH : (j + 1) * DH]


def softmax_low(scores):
    top = jnp.max(scores, axis=-1, keepdims=True)
    raised = jnp.exp(scores - top)
    return (raised * (1.0 / jnp.sum(raised, axis=-1, keepdims=True))).astype(BF)


def enc_attend(qkv, probs, mixed, bias, starts, heads, packed):
    blocks = packed // SLOT
    seg_keys = segment_of(iota((1, packed), 1), starts)

    @pl.loop(0, blocks)
    def _(i):
        rows = pl.ds(pl.multiple_of(i * SLOT, SLOT), SLOT)
        seg_rows = segment_of(iota((SLOT, 1), 0) + i * SLOT, starts)
        live = seg_rows == seg_keys
        for h in range(heads):
            scores = nt(qkv[h, rows, :], qkv[heads + h])
            add = jnp.concatenate([bias[h, j - i + blocks - 1] for j in range(blocks)], axis=1)
            low = softmax_low(jnp.where(live, scores + add, masked_score))
            probs[h, rows, :] = low
            mixed[rows, h * DH : (h + 1) * DH] = nn(low, qkv[2 * heads + h]).astype(BF)


def cross_attend(qkv, probs, mixed, lens, heads, packed):
    blocks = packed // SLOT
    starts = enc_starts(lens, blocks)
    place = iota((1, packed), 1)
    seg_keys = segment_of(place, starts)

    @pl.loop(0, blocks)
    def _(i):
        rows = pl.ds(pl.multiple_of(i * SLOT, SLOT), SLOT)
        live = seg_keys == i
        for h in range(heads):
            scores = nt(qkv[h, rows, :], qkv[heads + h])
            low = softmax_low(jnp.where(live, scores, masked_score))
            probs[h, rows, :] = low
            mixed[rows, h * DH : (h + 1) * DH] = nn(low, qkv[2 * heads + h]).astype(BF)


def self_attend(qkv, probs, mixed, bias, lens, heads, packed):
    place = iota((SLOT, SLOT), 1)
    lower = place <= iota((SLOT, SLOT), 0)

    @pl.loop(0, packed // SLOT)
    def _(i):
        rows = pl.ds(pl.multiple_of(i * SLOT, SLOT), SLOT)
        live = lower & (place < lens[0, i])
        for h in range(heads):
            scores = nt(qkv[h, rows, :], qkv[heads + h, rows, :])
            low = softmax_low(jnp.where(live, scores + bias[h], masked_score))
            probs[h, rows, :] = low
            mixed[rows, h * DH : (h + 1) * DH] = nn(low, qkv[2 * heads + h, rows, :]).astype(BF)


def score_grads(low, grad_mix, values):
    weights = low.astype(F32)
    part = weights * nt(grad_mix, values)
    return (part - weights * jnp.sum(part, axis=-1, keepdims=True)).astype(BF)


def full_attend_back(qkv, probs, grad_mixed, ds, grads, heads, packed):
    width = heads * DH

    @pl.loop(0, packed // SLOT)
    def _(i):
        rows = pl.ds(pl.multiple_of(i * SLOT, SLOT), SLOT)
        for h in range(heads):
            cols = slice(h * DH, (h + 1) * DH)
            low = score_grads(probs[h, rows, :], grad_mixed[rows, cols], qkv[2 * heads + h])
            ds[h, rows, :] = low
            grads[rows, cols] = nn(low, qkv[heads + h]).astype(BF)

    for h in range(heads):
        cols = slice(h * DH, (h + 1) * DH)
        grads[:, width + h * DH : width + (h + 1) * DH] = tn(ds[h], qkv[h]).astype(BF)
        grads[:, 2 * width + h * DH : 2 * width + (h + 1) * DH] = tn(
            probs[h], grad_mixed[:, cols]
        ).astype(BF)


def self_attend_back(qkv, probs, grad_mixed, ds_sum, grads, heads, packed):
    width = heads * DH
    for h in range(heads):
        ds_sum[h] = jnp.zeros((SLOT, SLOT), F32)

    @pl.loop(0, packed // SLOT)
    def _(i):
        rows = pl.ds(pl.multiple_of(i * SLOT, SLOT), SLOT)
        for h in range(heads):
            cols = slice(h * DH, (h + 1) * DH)
            prob = probs[h, rows, :]
            gm = grad_mixed[rows, cols]
            low = score_grads(prob, gm, qkv[2 * heads + h, rows, :])
            ds_sum[h] = ds_sum[h] + low.astype(F32)
            grads[rows, cols] = nn(low, qkv[heads + h, rows, :]).astype(BF)
            grads[rows, width + h * DH : width + (h + 1) * DH] = tn(low, qkv[h, rows, :]).astype(BF)
            grads[rows, 2 * width + h * DH : 2 * width + (h + 1) * DH] = tn(prob, gm).astype(BF)


def bucket_sums(pieces):
    return [jnp.sum(p, axis=1, keepdims=True) for p in pieces]


def put_table(out, lines, f, heads):
    lane = iota((BUCKETS, 128), 1)
    total = jnp.zeros((BUCKETS, 128), F32)
    for h in range(heads):
        summed = jnp.sum(lines[h], axis=1, keepdims=True)
        total = jnp.where(lane == f * heads + h, summed, total)
    out[...] = total


def dec_table_grad(ds_sum, line, out, f, heads):
    m = iota((SLOT, SLOT), 0) - iota((SLOT, SLOT), 1)
    limits = (0,) + causal_limits + (SLOT,)
    for b in range(BUCKETS):
        hit = (m >= limits[b]) & (m < limits[b + 1]) if b else m <= 0
        for h in range(heads):
            line[h, b : b + 1, :] = jnp.sum(
                jnp.where(hit, ds_sum[h], 0.0), axis=0, keepdims=True
            )
    put_table(out, [line[h] for h in range(heads)], f, heads)


def enc_table_grad(ds, ds_sum, line, out, f, heads, packed):
    blocks = packed // SLOT
    zero = jnp.zeros((SLOT, SLOT), F32)
    r = iota((SLOT, SLOT), 1) - iota((SLOT, SLOT), 0)
    limits = wide_limits + (10**6,)
    for h in range(heads):
        for slot in range(5):
            total = zero
            for i in range(blocks):
                for j in range(blocks):
                    if max(-2, min(2, j - i)) == slot - 2:
                        total = total + ds[h, i * SLOT : (i + 1) * SLOT, j * SLOT : (j + 1) * SLOT].astype(F32)
            ds_sum[h, slot] = total
    for h in range(heads):
        line[h] = jnp.zeros((BUCKETS, SLOT), F32)
        line[h, 0:1, :] = jnp.sum(jnp.where(r == 0, ds_sum[h, 2], 0.0), axis=0, keepdims=True)
    for b in range(15):
        low, high = limits[b], limits[b + 1]
        for side in (1, -1):
            rel = side * r
            hit_same = (rel >= low) & (rel < high)
            hit_next = (rel + SLOT >= low) & (rel + SLOT < high)
            row = 1 + b + (16 if side > 0 else 0)
            for h in range(heads):
                total = jnp.where(hit_same, ds_sum[h, 2], 0.0) + jnp.where(
                    hit_next, ds_sum[h, 2 + side], 0.0
                )
                if b == 14:
                    total = total + ds_sum[h, 2 + 2 * side]
                line[h, row : row + 1, :] = jnp.sum(total, axis=0, keepdims=True)
    put_table(out, [line[h] for h in range(heads)], f, heads)


def kernel_a(r, g):
    rows, f = g.rows, g.f
    packed = GROUP * rows
    heads = r.qkv_e.shape[0] // 3
    g.signal()
    own = g.slot(f)
    r.gath_a[own, :] = rms(r.enc_in[...].astype(F32), r.gains[0:1, :]).astype(BF)
    r.gath_c[own, :] = rms(r.dec_in[...].astype(F32), r.gains[3:4, :]).astype(BF)
    r.gath_g[own, :] = r.cot[...]
    ga, gc, gg = Gather(g, r.gath_a), Gather(g, r.gath_c), Gather(g, r.gath_g)
    xe, xd = Exchange(g, r.mixed_e, r.merged_e), Exchange(g, r.mixed_d, r.merged_d)
    g.wait()
    ga.start()
    gc.start()
    gg.start()
    enc_bias_blocks(r.tables, r.bias_e, f, heads, packed // SLOT)
    dec_bias_block(r.tables, r.bias_d, f, heads)
    ga.relay()
    ga.near()
    near, far = g.near_rows(), g.far_rows()
    put_heads(r.qkv_e, near, nn(r.gath_a[near, :], r.w_e[...]), 0)
    ga.far()
    put_heads(r.qkv_e, far, nn(r.gath_a[far, :], r.w_e[...]), 0)
    gc.relay()
    enc_attend(
        r.qkv_e, r.probs_e, r.mixed_e, r.bias_e, enc_starts(r.enc_lens, packed // SLOT), heads, packed
    )
    xe.start()
    gc.near()
    put_heads(r.qkv_d, near, nn(r.gath_c[near, :], r.w_d[...]), 0)
    gc.far()
    put_heads(r.qkv_d, far, nn(r.gath_c[far, :], r.w_d[...]), 0)
    self_attend(r.qkv_d, r.probs_d, r.mixed_d, r.bias_d, r.dec_lens, heads, packed)
    xd.start()
    gg.relay()
    xe.recv()
    r.x1[...] = r.enc_in[...].astype(F32) + merged_out(r.merged_e, r.wo_e)
    xd.recv()
    r.d1[...] = r.dec_in[...].astype(F32) + merged_out(r.merged_d, r.wo_d)
    gg.near()
    gg.far()
    for item in (ga, gc, gg, xe, xd):
        item.done()


def kernel_b(r, g):
    rows, f = g.rows, g.f
    packed = GROUP * rows
    heads = r.qkv_c.shape[0] // 3
    g.signal()
    own = g.slot(f)
    r.gath_b[own, :] = rms(r.x1[...], r.gains[1:2, :]).astype(BF)
    r.gath_d[own, :] = rms(r.d1[...], r.gains[4:5, :]).astype(BF)
    gb, gd, gm = Gather(g, r.gath_b), Gather(g, r.gath_d), Gather(g, r.gath_m)
    rs = scatter_of(g, r, "rs")
    xc = Exchange(g, r.mixed_c, r.merged_c)
    near, far = g.near_rows(), g.far_rows()
    g.wait()
    gb.start()
    gd.start()

    def hidden_of(part):
        pre = nn(r.gath_b[part, :], r.w_in[...])
        r.pre[part, :] = pre
        r.hidden[part, :] = (pre * gelu_cdf(pre)).astype(BF)

    gb.near()
    hidden_of(near)
    gb.relay()
    gb.far()
    hidden_of(far)
    rs.put_far(nn(r.hidden[far, :], r.w_down[...]))
    rs.put_near(nn(r.hidden[near, :], r.w_down[...]))
    rs.relay()
    gd.relay()
    gd.near()
    put_heads(r.qkv_c, near, nn(r.gath_d[near, :], r.w_q[...]), 0)
    gd.far()
    put_heads(r.qkv_c, far, nn(r.gath_d[far, :], r.w_q[...]), 0)
    x2 = r.x1[...] + rs.result()
    r.x2[...] = x2
    r.gath_m[own, :] = rms(x2, r.gains[2:3, :]).astype(BF)
    gm.start()
    gm.near()
    put_heads(r.qkv_c, near, nn(r.gath_m[near, :], r.w_kv[...]), heads)
    gm.relay()
    gm.far()
    put_heads(r.qkv_c, far, nn(r.gath_m[far, :], r.w_kv[...]), heads)
    cross_attend(r.qkv_c, r.probs_c, r.mixed_c, r.enc_lens, heads, packed)
    xc.start()
    xc.recv()
    r.d2[...] = r.d1[...] + merged_out(r.merged_c, r.wo_c)
    for item in (gb, gd, gm, rs, xc):
        item.done()


def kernel_c(r, g):
    rows, f = g.rows, g.f
    g.signal()
    own = g.slot(f)
    r.gath_e[own, :] = rms(r.d2[...], r.gains[5:6, :]).astype(BF)
    ge = Gather(g, r.gath_e)
    rb, rf = scatter_of(g, r, "rb"), scatter_of(g, r, "rf")
    near, far = g.near_rows(), g.far_rows()
    g.wait()
    ge.start()

    def backward_of(part):
        pre = nn(r.gath_e[part, :], r.w_in[...])
        cdf = gelu_cdf(pre)
        r.hidden[part, :] = (pre * cdf).astype(BF)
        back = r.grad_hidden[part, :].astype(F32) * gelu_slope(pre, cdf)
        r.grad_pre[part, :] = back.astype(BF)

    r.grad_hidden[near, :] = nt(r.gath_g[near, :], r.w_down[...]).astype(BF)
    r.grad_hidden[far, :] = nt(r.gath_g[far, :], r.w_down[...]).astype(BF)
    ge.near()
    backward_of(near)
    ge.relay()
    ge.far()
    backward_of(far)
    rb.put_far(nt(r.grad_pre[far, :], r.w_in[...]))
    rb.put_near(nt(r.grad_pre[near, :], r.w_in[...]))
    rb.relay()
    rf.put_far(nn(r.hidden[far, :], r.w_down[...]))
    rf.put_near(nn(r.hidden[near, :], r.w_down[...]))
    rf.relay()
    r.unit_in[...] = tn(r.gath_e[...], r.grad_pre[...]).astype(BF)
    r.unit_down[...] = tn(r.gath_g[...], r.hidden[...]).astype(BF)
    d2 = r.d2[...]
    grad, gain = rms_back(d2, r.gains[5:6, :], rb.result())
    r.g2[...] = r.cot[...].astype(F32) + grad
    r.gain[...] = gain
    r.dec_out[...] = (d2 + rf.result()).astype(BF)
    for item in (ge, rb, rf):
        item.done()


def kernel_d(r, g):
    rows, f = g.rows, g.f
    packed = GROUP * rows
    heads = r.qkv_c.shape[0] // 3
    width = heads * DH
    g.signal()
    own = g.slot(f)
    r.gath_g2[own, :] = r.g2[...].astype(BF)
    gg = Gather(g, r.gath_g2)
    rm, rq = scatter_of(g, r, "rm"), scatter_of(g, r, "rq")
    near, far = g.near_rows(), g.far_rows()
    g.wait()
    gg.start()
    gg.near()
    r.grad_mixed[near, :] = nt(r.gath_g2[near, :], r.wo_part[...]).astype(BF)
    gg.relay()
    gg.far()
    r.grad_mixed[far, :] = nt(r.gath_g2[far, :], r.wo_part[...]).astype(BF)
    full_attend_back(r.qkv_c, r.probs_c, r.grad_mixed, r.ds, r.grads, heads, packed)
    rm.put_far(nt(r.grads[far, width:], r.w_kv[...]))
    rm.put_near(nt(r.grads[near, width:], r.w_kv[...]))
    rm.relay()
    rq.put_far(nt(r.grads[far, :width], r.w_q[...]))
    rq.put_near(nt(r.grads[near, :width], r.w_q[...]))
    rq.relay()
    r.unit[:, :width] = tn(r.gath_d[...], r.grads[:, :width]).astype(BF)
    r.unit[:, width : 3 * width] = tn(r.gath_m[...], r.grads[:, width:]).astype(BF)
    r.unit[:, 3 * width :] = tn(r.gath_g2[...], r.mixed_c[...]).astype(BF)
    grad, gain = rms_back(r.x2[...], r.gains[2:3, :], rm.result())
    r.g_last[...] = grad
    r.gain_m[...] = gain
    grad, gain = rms_back(r.d1[...], r.gains[4:5, :], rq.result())
    r.g1[...] = r.g2[...] + grad
    r.gain_d[...] = gain
    for item in (gg, rm, rq):
        item.done()


def kernel_e(r, g):
    rows, f = g.rows, g.f
    packed = GROUP * rows
    heads = r.qkv_d.shape[0] // 3
    width = heads * DH
    g.signal()
    own = g.slot(f)
    r.gath_l[own, :] = r.g_last[...].astype(BF)
    r.gath_g1[own, :] = r.g1[...].astype(BF)
    gl, gg = Gather(g, r.gath_l), Gather(g, r.gath_g1)
    rf, rd = scatter_of(g, r, "rf"), scatter_of(g, r, "rd")
    near, far = g.near_rows(), g.far_rows()
    g.wait()
    gl.start()
    gg.start()

    def backward_of(part):
        pre = r.pre[part, :]
        back = nt(r.gath_l[part, :], r.w_down[...]).astype(BF).astype(F32) * gelu_slope(pre, gelu_cdf(pre))
        r.grad_pre[part, :] = back.astype(BF)

    gl.near()
    backward_of(near)
    gl.relay()
    gl.far()
    backward_of(far)
    rf.put_far(nt(r.grad_pre[far, :], r.w_in[...]))
    rf.put_near(nt(r.grad_pre[near, :], r.w_in[...]))
    rf.relay()
    gg.relay()
    gg.near()
    r.grad_mixed[near, :] = nt(r.gath_g1[near, :], r.wo_part[...]).astype(BF)
    gg.far()
    r.grad_mixed[far, :] = nt(r.gath_g1[far, :], r.wo_part[...]).astype(BF)
    self_attend_back(r.qkv_d, r.probs_d, r.grad_mixed, r.ds_sum, r.grads, heads, packed)
    rd.put_far(nt(r.grads[far, :], r.w_d[...]))
    rd.put_near(nt(r.grads[near, :], r.w_d[...]))
    rd.relay()
    grad, gain = rms_back(r.x1[...], r.gains[1:2, :], rf.result())
    r.g_mid[...] = r.g_last[...] + grad
    r.gain_b[...] = gain
    r.unit_in[...] = tn(r.gath_b[...], r.grad_pre[...]).astype(BF)
    r.unit_down[...] = tn(r.gath_l[...], r.hidden[...]).astype(BF)
    r.unit[:, : 3 * width] = tn(r.gath_c[...], r.grads[...]).astype(BF)
    r.unit[:, 3 * width :] = tn(r.gath_g1[...], r.mixed_d[...]).astype(BF)
    dec_table_grad(r.ds_sum, r.line, r.table, f, heads)
    grad, gain = rms_back(r.dec_in[...].astype(F32), r.gains[3:4, :], rd.result())
    r.dec_grad[...] = (r.g1[...] + grad).astype(BF)
    r.gain_c[...] = gain
    for item in (gl, gg, rf, rd):
        item.done()


def kernel_f(r, g):
    rows, f = g.rows, g.f
    packed = GROUP * rows
    heads = r.qkv_e.shape[0] // 3
    width = heads * DH
    g.signal()
    own = g.slot(f)
    r.gath_gm[own, :] = r.g_mid[...].astype(BF)
    gg = Gather(g, r.gath_gm)
    rs = scatter_of(g, r, "rs")
    near, far = g.near_rows(), g.far_rows()
    g.wait()
    gg.start()
    gg.near()
    r.grad_mixed[near, :] = nt(r.gath_gm[near, :], r.wo_part[...]).astype(BF)
    gg.relay()
    gg.far()
    r.grad_mixed[far, :] = nt(r.gath_gm[far, :], r.wo_part[...]).astype(BF)
    full_attend_back(r.qkv_e, r.probs_e, r.grad_mixed, r.ds, r.grads, heads, packed)
    rs.put_far(nt(r.grads[far, :], r.w_e[...]))
    rs.put_near(nt(r.grads[near, :], r.w_e[...]))
    rs.relay()
    r.unit[:, : 3 * width] = tn(r.gath_a[...], r.grads[...]).astype(BF)
    r.unit[:, 3 * width :] = tn(r.gath_gm[...], r.mixed_e[...]).astype(BF)
    enc_table_grad(r.ds, r.ds_sum, r.line, r.table, f, heads, packed)
    grad, gain = rms_back(r.enc_in[...].astype(F32), r.gains[0:1, :], rs.result())
    r.enc_grad[...] = (r.g_mid[...] + grad).astype(BF)
    r.gain[...] = gain
    for item in (gg, rs):
        item.done()


def on_device(
    enc_in,
    dec_in,
    cotangent,
    enc_lengths,
    dec_lengths,
    qk_weights,
    v_weights,
    out_weights,
    ffn_in,
    ffn_out,
    bias_tables,
    gains,
):
    group_size = lax.axis_size("ffn")
    f = lax.axis_index("ffn")
    rows, model = enc_in.shape
    packed = rows * group_size
    width = qk_weights.shape[3] // group_size
    heads = width // DH
    hidden = ffn_in.shape[2]
    side = SLOT

    def cut(weights, axis):
        return lax.dynamic_slice_in_dim(weights, f * width, width, axis)

    qk_cut, v_cut = cut(qk_weights, 3), cut(v_weights, 2)
    w_qkv = [jnp.concatenate([qk_cut[l, 0], qk_cut[l, 1], v_cut[l]], axis=1) for l in range(2)]
    w_q, w_kv = qk_cut[2, 0], jnp.concatenate([qk_cut[2, 1], v_cut[2]], axis=1)
    wo_part = cut(out_weights, 1)

    low = lambda *shape: (shape, BF)
    wide = lambda *shape: (shape, F32)
    v = lambda a: (a, "v")
    s = lambda a: (a, "s")
    call = functools.partial(run, rows=rows)

    a = call(
        "self_attentions", 1, kernel_a,
        dict(
            enc_in=v(enc_in), dec_in=v(dec_in), cot=v(cotangent), gains=v(gains), tables=s(bias_tables),
            enc_lens=s(enc_lengths), dec_lens=s(dec_lengths), w_e=v(w_qkv[0]), w_d=v(w_qkv[1]),
            wo_e=v(out_weights[0]), wo_d=v(out_weights[1]),
        ),
        dict(
            gath_a=low(packed, model), gath_c=low(packed, model), gath_g=low(packed, model),
            qkv_e=low(3 * heads, packed, DH), qkv_d=low(3 * heads, packed, DH),
            probs_e=low(heads, packed, packed), probs_d=low(heads, packed, side),
            mixed_e=low(packed, width), mixed_d=low(packed, width),
            x1=wide(rows, model), d1=wide(rows, model),
        ),
        dict(
            bias_e=wide(heads, 2 * (packed // side) - 1, side, side), bias_d=wide(heads, side, side),
            merged_e=low(GROUP, rows, width), merged_d=low(GROUP, rows, width),
        ),
        15,
    )
    b = call(
        "encoder_ffn_cross", 2, kernel_b,
        dict(
            x1=v(a["x1"]), d1=v(a["d1"]), gains=v(gains), enc_lens=s(enc_lengths),
            w_in=v(ffn_in[0]), w_down=v(ffn_out[0]), w_q=v(w_q), w_kv=v(w_kv), wo_c=v(out_weights[2]),
        ),
        dict(
            gath_b=low(packed, model), gath_d=low(packed, model), gath_m=low(packed, model),
            pre=wide(packed, hidden), hidden=low(packed, hidden),
            qkv_c=low(3 * heads, packed, DH), probs_c=low(heads, packed, packed),
            mixed_c=low(packed, width), x2=wide(rows, model), d2=wide(rows, model),
        ),
        dict(merged_c=low(GROUP, rows, width), **scatter_scratch("rs", rows, model)),
        15,
    )
    c = call(
        "decoder_ffn", 3, kernel_c,
        dict(
            d2=v(b["d2"]), cot=v(cotangent), gath_g=v(a["gath_g"]), gains=v(gains),
            w_in=v(ffn_in[1]), w_down=v(ffn_out[1]),
        ),
        dict(
            dec_out=low(rows, model), g2=wide(rows, model), gain=wide(1, model),
            unit_in=low(model, hidden), unit_down=low(model, hidden),
        ),
        dict(
            gath_e=low(packed, model), hidden=low(packed, hidden), grad_hidden=low(packed, hidden),
            grad_pre=low(packed, hidden),
            **scatter_scratch("rb", rows, model), **scatter_scratch("rf", rows, model),
        ),
        9,
    )
    d = call(
        "cross_back", 4, kernel_d,
        dict(
            g2=v(c["g2"]), x2=v(b["x2"]), d1=v(a["d1"]), gains=v(gains), gath_d=v(b["gath_d"]),
            gath_m=v(b["gath_m"]), qkv_c=v(b["qkv_c"]), probs_c=v(b["probs_c"]), mixed_c=v(b["mixed_c"]),
            w_q=v(w_q), w_kv=v(w_kv), wo_part=v(wo_part[2]),
        ),
        dict(
            g_last=wide(rows, model), g1=wide(rows, model), unit=low(model, 4 * width),
            gain_m=wide(1, model), gain_d=wide(1, model),
        ),
        dict(
            gath_g2=low(packed, model), grad_mixed=low(packed, width), ds=low(heads, packed, packed),
            grads=low(packed, 3 * width),
            **scatter_scratch("rm", rows, model), **scatter_scratch("rq", rows, model),
        ),
        9,
    )
    e = call(
        "encoder_ffn_self_back", 5, kernel_e,
        dict(
            g_last=v(d["g_last"]), g1=v(d["g1"]), x1=v(a["x1"]), dec_in=v(dec_in), gains=v(gains),
            gath_b=v(b["gath_b"]), gath_c=v(a["gath_c"]), pre=v(b["pre"]), hidden=v(b["hidden"]),
            w_in=v(ffn_in[0]), w_down=v(ffn_out[0]), qkv_d=v(a["qkv_d"]), probs_d=v(a["probs_d"]),
            mixed_d=v(a["mixed_d"]), w_d=v(w_qkv[1]), wo_part=v(wo_part[1]),
        ),
        dict(
            g_mid=wide(rows, model), dec_grad=low(rows, model), unit_in=low(model, hidden),
            unit_down=low(model, hidden), unit=low(model, 4 * width), gain_b=wide(1, model),
            gain_c=wide(1, model), table=wide(BUCKETS, 128),
        ),
        dict(
            gath_l=low(packed, model), gath_g1=low(packed, model), grad_pre=low(packed, hidden),
            grad_mixed=low(packed, width), grads=low(packed, 3 * width), ds_sum=wide(heads, side, side),
            line=wide(heads, BUCKETS, side),
            **scatter_scratch("rf", rows, model), **scatter_scratch("rd", rows, model),
        ),
        12,
    )
    h = call(
        "encoder_self_back", 6, kernel_f,
        dict(
            g_mid=v(e["g_mid"]), enc_in=v(enc_in), gains=v(gains), gath_a=v(a["gath_a"]),
            qkv_e=v(a["qkv_e"]), probs_e=v(a["probs_e"]), mixed_e=v(a["mixed_e"]), w_e=v(w_qkv[0]),
            wo_part=v(wo_part[0]),
        ),
        dict(
            enc_grad=low(rows, model), unit=low(model, 4 * width), gain=wide(1, model),
            table=wide(BUCKETS, 128),
        ),
        dict(
            gath_gm=low(packed, model), grad_mixed=low(packed, width), ds=low(heads, packed, packed),
            grads=low(packed, 3 * width), ds_sum=wide(heads, 5, side, side), line=wide(heads, BUCKETS, side),
            **scatter_scratch("rs", rows, model),
        ),
        6,
    )

    def summed(units):
        return lax.psum_scatter(jnp.stack(units), "tok", scatter_dimension=1, tiled=True)

    early = summed([c["unit_in"], c["unit_down"], d["unit"]]).astype(F32)
    late = summed([e["unit"], e["unit_in"], e["unit_down"], h["unit"]]).astype(F32)
    dec_up, dec_down, cross = early[0], early[1], early[2]
    self_unit, enc_up, enc_down, enc_unit = late[0], late[1], late[2], late[3]
    layers = (enc_unit, self_unit, cross)
    qk_grad = jnp.stack([jnp.stack([u[:, :width], u[:, width : 2 * width]]) for u in layers])
    v_grad = jnp.stack([u[:, 2 * width : 3 * width] for u in layers])
    out_grad = jnp.stack([u[:, 3 * width :].T for u in layers])
    up_grad = jnp.stack([enc_up, dec_up])
    down_grad = jnp.stack([enc_down.T, dec_down.T])
    gain_terms = jnp.concatenate(
        [h["gain"], e["gain_b"], d["gain_m"], e["gain_c"], d["gain_d"], c["gain"]], axis=0
    )
    table_terms = jnp.stack([h["table"], e["table"]])
    gain_grad, table_grad = lax.psum((gain_terms, table_terms), ("tok", "ffn"))
    return (
        c["dec_out"],
        h["enc_grad"],
        e["dec_grad"],
        qk_grad,
        v_grad,
        out_grad,
        up_grad,
        down_grad,
        table_grad[:, :, : bias_tables.shape[2]],
        gain_grad,
        gain_grad[5],
    )


def solution(mesh):
    placed = (
        P(("tok", "ffn"), None),
        P(("tok", "ffn"), None),
        P(("tok", "ffn"), None),
        P("tok", None),
        P("tok", None),
        P(),
        P(),
        P(),
        P(None, None, "ffn"),
        P(None, "ffn", None),
        P(),
        P(),
    )
    return jax.shard_map(
        on_device,
        mesh=mesh,
        in_specs=placed,
        out_specs=(
            P(("tok", "ffn"), None),
            P(("tok", "ffn"), None),
            P(("tok", "ffn"), None),
            P(None, None, "tok", "ffn"),
            P(None, "tok", "ffn"),
            P(None, "ffn", "tok"),
            P(None, "tok", "ffn"),
            P(None, "ffn", "tok"),
            P(),
            P(),
            P(),
        ),
        check_vma=False,
    )
```

time: 1300 us -> 385 us (0.30)
  waiting for transfers between devices: 510 us -> 60.2 us
  local copies, waits for them, and re-layouts: 353 us -> 23.6 us
  Pallas kernels: 0 us -> 221 us
  matrix products: 163 us -> 0 us
  starting transfers between devices: 86 us -> 0.08 us
  other arithmetic: 69 us -> 16.9 us
  blocking collectives: 94.7 us -> 43.4 us
    reduce_scatter x7 -> x2, waiting for transfers between devices: 460 us -> 60.2 us  [summed(): lax.psum_scatter(jnp.stack(units), 'tok', scatter_dimension=1, tiled=True)]
    pallas_call x0 -> x6, Pallas kernels: none -> 221 us  [run(): pl.pallas_call(kernel, out_shape=[jax.ShapeDtypeStruct(*outs[n]) for n in...]
    dot_general x70 -> x0, matrix products: 163 us -> none  [the longest x34 70.5 us: product(): lax.dot_general(left, right, contract, preferred_element_type=jnp.float32)]
    unnamed x303 -> x48, local copies, waits for them, and re-layouts: 163 us -> 5.05 us
    all_to_all x23 -> x0, starting transfers between devices: 85.1 us -> none  [the longest x3 12.1 us: attention_backward(): lax.all_to_all(head_values, 'ffn', split_axis=0, concat_axis=1, tiled=True)]
    reshape x22 -> x0, local copies, waits for them, and re-layouts: 65.5 us -> none  [the longest x4 60.5 us: bias_block(): spread[:, :block_rows * (line_width - 1)]]
    all_to_all x84 -> x0, local copies, waits for them, and re-layouts: 57.3 us -> none  [the longest x12 15.5 us: attention_backward(): lax.all_to_all(head_query, 'ffn', split_axis=0, concat_axis=1, tiled=True)]
    all_to_all x23 -> x0, waiting for transfers between devices: 50 us -> none  [the longest x3 14.7 us: attention_backward(): lax.all_to_all(grad_merged, 'ffn', split_axis=1, concat_axis=0, tiled=True)]
  transfers between devices with their start and end apart: 32 -> 2, of which waited for: 20 -> 1; matrix products, arithmetic and copies ran while one was open for 38% -> 2% of each run, Pallas kernels for 0% -> 18%
where the time goes in v1:
time: 385 us; the launch traced here: 379 us
  Pallas kernels  221 us (57%)
  waiting for transfers between devices  60.2 us (16%)
  blocking collectives  43.4 us (11%)
  local copies, waits for them, and re-layouts  23.6 us (6%)
  other arithmetic  16.9 us (4%)
  between operations  14.6 us (4%)
    pallas_call x6, Pallas kernels, run(): pl.pallas_call(kernel, out_shape=[jax.ShapeDtypeStruct(*outs[n]) for n in...  221 us
    reduce_scatter x2, waiting for transfers between devices, summed(): lax.psum_scatter(jnp.stack(units), 'tok', scatter_dimension=1, tiled=True)  60.2 us
    psum x1, blocking collectives, on_device(): gain_grad, table_grad = lax.psum((gain_terms, table_terms), ('tok', 'ffn'))  43.4 us
  transfers between devices with their start and end apart: 2, of which 1 were waited for; matrix products, arithmetic and copies ran while one was open for 2% of the time, Pallas kernels for 18%

profile of v1, /device:TPU:0, one launch (start us, length us, event | category | flops | bytes accessed | tf_op | source)
XLA Modules:
  0.0 379.4 jit_solution(15026012550991919629)
XLA Ops:
  7.2 0.0 reduce-scatter.5.cloned.1.call-start
  7.2 3.8 %slice_bitcast_fusion.2 = (bf16[768,768]{1,0:T(8,128)(2,1)}, bf16[768,768]{1,0:T(8,128)(2,1)}, bf16[768,768]{1,0:T(8,128)(2,1)}) fusion(bf16[3,768,768]{2,1,0:T(8,128)(2,1)} %param.19), kind=kLoop, calls=%fused_computation.4 | loop fusion | bytes 7077888 | tf_op jit(solution)/shard_map/squeeze | solution.py:795
  11.1 2.1 dynamic-slice_bitcast_fusion.9
  13.1 4.5 %dynamic-slice_bitcast_fusion.1 = (bf16[768,192]{1,0:T(8,128)(2,1)}, bf16[768,192]{1,0:T(8,128)(2,1)}, bf16[768,192]{1,0:T(8,128)(2,1)}, bf16[768,192]{1,0:T(8,1...) fusion(bf16[3,2,768,768]{3,2,1,0:T(8,128)(2,1)} %param.17, s32[]{:T(128)S(6)} %add.20, s32[]{:T(128)S(6)} %add.15, ...), kind=kLoop, calls=%fused_computation.16 | loop fusion | bytes 3538956 | tf_op jit(solution)/shard_map/squeeze | solution.py:762
  17.7 2.1 dynamic-slice_bitcast_fusion
  19.8 0.7 copy.23.refs_4_
  20.5 2.0 pad_maximum_fusion.4.refs_7_.refs_10_
  22.5 0.0 copy-start.4
  22.5 4.0 %slice_bitcast_fusion = (bf16[768,768]{1,0:T(8,128)(2,1)}, bf16[768,768]{1,0:T(8,128)(2,1)}, bf16[768,768]{1,0:T(8,128)(2,1)}, bf16[768,768]{1,0:T(8,128)(2,1)}) fusion(bf16[2,768,768]{2,1,0:T(8,128)(2,1)S(1)} %copy-done, bf16[2,768,768]{2,1,0:T(8,128)(2,1)} %param.20), kind=kLoop, calls=%fused_computation.2 | loop fusion | bytes 9437184 | tf_op jit(solution)/shard_map/squeeze | solution.py:810
  26.5 2.1 pad_maximum_fusion.2
  28.6 41.8 %self_attentions.1 = (bf16[640,768]{1,0:T(8,128)(2,1)}, bf16[640,768]{1,0:T(8,128)(2,1)}, bf16[640,768]{1,0:T(8,128)(2,1)}, bf16[9,640,64]{2,1,0:T(8,128)(2,1)},...) custom-call(bf16[160,768]{1,0:T(8,128)(2,1)} %refs_1_.5, ...), custom_call_target="tpu_custom_call" | custom-call | tf_op jit(solution)/shard_map/self_attentions/pallas_call | solution.py:241
  70.4 45.6 %encoder_ffn_cross.1 = (bf16[640,768]{1,0:T(8,128)(2,1)}, bf16[640,768]{1,0:T(8,128)(2,1)}, bf16[640,768]{1,0:T(8,128)(2,1)}, f32[640,768]{1,0:T(8,128)}, bf16[6...) custom-call(f32[160,768]{1,0:T(8,128)} %get-tuple-element.54.refs_0_, ...), custom_call_target="tpu_custom_call" | custom-call | tf_op jit(solution)/shard_map/encoder_ffn_cross/pallas_call | solution.py:241
  116.1 29.2 %decoder_ffn.1 = (bf16[160,768]{1,0:T(8,128)(2,1)}, f32[160,768]{1,0:T(8,128)}, f32[1,768]{1,0:T(1,128)}, bf16[768,768]{1,0:T(8,128)(2,1)}, bf16[768,768]{1,0:T(8,128)(2,1)}) custom-call(f32[160,768]{1,0:T(8,128)} %get-tuple-element.56.refs_0_, bf16[160,768]{1,0:T(8,128)(2,1)} %refs_1_.4, bf16[640,768]{1,0:T(8,128)(2,1)} %get-tuple-element.57.refs_2_, ...), custom_call_target="tpu_custom_call" | custom-call | tf_op jit(solution)/shard_map/decoder_ffn/pallas_call | solution.py:241
  145.3 36.2 %cross_back.1 = (f32[160,768]{1,0:T(8,128)}, f32[160,768]{1,0:T(8,128)}, bf16[768,768]{1,0:T(8,128)(2,1)}, f32[1,768]{1,0:T(1,128)}, f32[1,768]{1,0:T(1,128)}) custom-call(f32[160,768]{1,0:T(8,128)} %get-tuple-element.59.refs_0_, f32[160,768]{1,0:T(8,128)} %get-tuple-element.60.refs_1_, f32[160,768]{1,0:T(8,128)} %get-tuple-element.55.refs_1_.refs_2_, ...), custom_call_target="tpu_custom_call" | custom-call | tf_op jit(solution)/shard_map/cross_back/pallas_call | solution.py:241
  181.5 3.2 pad_maximum_fusion.1
  184.7 0.0 reduce-scatter.5.cloned.1.call-update
  184.8 0.0 reduce-scatter.3.cloned.1.call-start
  184.8 37.5 %encoder_ffn_self_back.1 = (f32[160,768]{1,0:T(8,128)}, bf16[160,768]{1,0:T(8,128)(2,1)}, bf16[768,768]{1,0:T(8,128)(2,1)}, bf16[768,768]{1,0:T(8,128)(2,1)}, bf...) custom-call(f32[160,768]{1,0:T(8,128)} %get-tuple-element.66.refs_0_, ...), custom_call_target="tpu_custom_call" | custom-call | tf_op jit(solution)/shard_map/encoder_ffn_self_back/pallas_call | solution.py:241
  222.4 30.4 %encoder_self_back.1 = (bf16[160,768]{1,0:T(8,128)(2,1)}, bf16[768,768]{1,0:T(8,128)(2,1)}, f32[1,768]{1,0:T(1,128)}, f32[32,128]{1,0:T(8,128)}) custom-call(f32[160,768]{1,0:T(8,128)} %get-tuple-element.75.refs_0_, bf16[160,768]{1,0:T(8,128)(2,1)} %refs_1_.5, f32[6,768]{1,0:T(8,128)} %refs_2_.5, bf16[640,768]{1,0:T(8,128)(2,1)} %get-tuple-element.76.refs_3_, ...), custom_call_target="tpu_custom_call" | custom-call | tf_op jit(solution)/shard_map/encoder_self_back/pallas_call | solution.py:241
  252.8 3.9 %pad_maximum_fusion = bf16[4,768,768]{2,1,0:T(8,128)(2,1)} fusion(bf16[1,768,768]{2,1,0:T(8,128)(2,1)} %bitcast.105, bf16[1,768,768]{2,1,0:T(8,128)(2,1)} %bitcast.103, bf16[1,768,768]{2,1,0:T(8,128)(2,1)S(1)} %bitcast.102, bf16[1,768,768]{2,1,0:T(8,128)(2,1)} %bitcast.104), kind=kLoop, calls=%fused_computation | loop fusion | flops 7077888 | bytes 9437184 | tf_op jit(solution)/shard_map/stack | solution.py:882
  256.7 0.0 reduce-scatter.3.cloned.1.call-update
  256.8 0.6 copy-done.14
  257.3 0.0 copy-done.15
  257.4 0.0 copy-done.16
  257.4 0.0 copy-done.17
  257.4 0.0 copy-done.19
  257.4 0.0 copy-done.11
  257.4 0.0 copy-done.12
  257.5 43.4 %all-reduce = (f32[2,32,128]{2,1,0:T(8,128)S(1)}, f32[6,768]{1,0:T(8,128)S(1)}) all-reduce(f32[2,32,128]{2,1,0:T(8,128)S(1)} %pad_maximum_fusion.10, f32[6,768]{1,0:T(8,128)S(1)} %concatenate.15), channel_id=1, replica_groups=mesh['tok'=8,'ffn'=4] {'tok','ffn'}, use_global_device_ids=true, to_apply=%region_2.0 | all-reduce | flops 12800 | bytes 102400 | tf_op jit(solution)/shard_map/psum | solution.py:898
  300.8 0.0 copy-start.20
  300.9 0.7 copy.25
  301.5 0.6 slice_reduce_fusion
  302.1 1.1 convert_element_type.7
  303.2 0.9 slice.178
  304.2 0.1 slice_bitcast_fusion.12
  304.4 60.2 %reduce-scatter.3.cloned.1.call-done = bf16[4,96,768]{2,1,0:T(8,128)(2,1)} async-done(((bf16[4,768,768]{2,1,0:T(8,128)(2,1)}), bf16[4,96,768]{2,1,0:T(8,128)(2,1)}) %reduce-scatter.3.cloned.1.call-update) | async-done | bytes 589840 | tf_op jit(solution)/shard_map/reduce_scatter | solution.py:882
  364.5 1.2 convert_element_type.6
  365.7 0.1 slice_bitcast_fusion.8
  365.8 0.1 slice_bitcast_fusion.14
  365.9 0.1 slice_bitcast_fusion.13
  366.0 0.9 copy.24
  366.9 0.9 pad_maximum_fusion.7
  367.8 0.9 pad_maximum_fusion.6
  368.7 0.7 pad_maximum_fusion.8
  369.4 0.9 pad_maximum_fusion.5
  370.3 0.7 copy.29
  371.0 0.7 copy.30
  371.7 0.7 copy.31
  (42 shorter events, 0.2 us)
Async XLA Ops:
  7.2 295.0 %reduce-scatter.5.cloned.1.call-start = ((), (), s32[]{:S(2)}) async-start(), calls=%async_computation.3 | async-start | bytes 3981312 | tf_op jit(solution)/shard_map/reduce_scatter | solution.py:882
  13.1 6.6 %copy-start.13 = (f32[2,32,12]{1,0,2:T(2,128)S(1)}, f32[2,32,12]{1,0,2:T(2,128)}, u32[]{:S(2)}) copy-start(f32[2,32,12]{1,0,2:T(2,128)} %param.22) | copy-start | bytes 9220
  17.7 4.8 %copy-start = (bf16[2,768,768]{2,1,0:T(8,128)(2,1)S(1)}, bf16[2,768,768]{2,1,0:T(8,128)(2,1)}, u32[]{:S(2)}) copy-start(bf16[2,768,768]{2,1,0:T(8,128)(2,1)} %param.21) | copy-start | bytes 7077892
  22.5 4.0 %copy-start.1 = (bf16[768,192]{1,0:T(8,128)(2,1)S(1)}, bf16[768,192]{1,0:T(8,128)(2,1)}, u32[]{:S(2)}) copy-start(bf16[768,192]{1,0:T(8,128)(2,1)} %get-tuple-element.112) | copy-start | bytes 884740
  22.5 4.0 %copy-start.2 = (bf16[768,192]{1,0:T(8,128)(2,1)S(1)}, bf16[768,192]{1,0:T(8,128)(2,1)}, u32[]{:S(2)}) copy-start(bf16[768,192]{1,0:T(8,128)(2,1)} %get-tuple-element.113) | copy-start | bytes 884740
  22.5 4.0 %copy-start.3 = (bf16[768,192]{1,0:T(8,128)(2,1)S(1)}, bf16[768,192]{1,0:T(8,128)(2,1)}, u32[]{:S(2)}) copy-start(bf16[768,192]{1,0:T(8,128)(2,1)} %get-tuple-element.114) | copy-start | bytes 884740
  22.5 4.0 %copy-start.4 = (bf16[768,192]{1,0:T(8,128)(2,1)S(1)}, bf16[768,192]{1,0:T(8,128)(2,1)}, u32[]{:S(2)}) copy-start(bf16[768,192]{1,0:T(8,128)(2,1)} %get-tuple-element.115) | copy-start | bytes 884740
  145.3 36.2 %copy-start.7 = (bf16[768,768]{1,0:T(8,128)(2,1)S(1)}, bf16[768,768]{1,0:T(8,128)(2,1)}, u32[]{:S(2)}) copy-start(bf16[768,768]{1,0:T(8,128)(2,1)} %get-tuple-element.86) | copy-start | bytes 3538948
  184.8 179.8 %reduce-scatter.3.cloned.1.call-start = ((), (), s32[]{:S(2)}) async-start(), calls=%async_computation.2 | async-start | bytes 5308416 | tf_op jit(solution)/shard_map/reduce_scatter | solution.py:882
  222.4 30.4 %copy-start.6 = (bf16[768,768]{1,0:T(8,128)(2,1)S(1)}, bf16[768,768]{1,0:T(8,128)(2,1)}, u32[]{:S(2)}) copy-start(bf16[768,768]{1,0:T(8,128)(2,1)} %get-tuple-element.83) | copy-start | bytes 3538948
  256.7 0.7 copy-start.14
  256.7 0.7 copy-start.15
  256.7 0.7 copy-start.16
  256.7 0.7 copy-start.17
  256.7 0.7 copy-start.18
  256.7 0.7 copy-start.19
  256.7 0.7 copy-start.11
  256.7 0.7 copy-start.12
  300.8 3.5 copy-start.20
  365.8 2.0 copy-start.5
  367.8 2.5 copy-start.8
  367.8 3.2 copy-start.10
  368.7 3.0 copy-start.9
Sparse Core Ops, SparseCore 0:
  184.9 80.3 reduce-scatter.4
  269.0 95.5 reduce-scatter.2
